TPU v7x, 32 devices: a whole 2x2x4 slice. The times are simulated.
32 devices in a mesh: gx: 16 (over z, y, x), gy: 2 (over core).
Axes of the slice: x: 2, y: 2, z: 4, core: 2. Of those that a mesh axis runs over, the one named last changes fastest.
Arguments:
- classes: int32 [128, 64, 128], P('gx', 'gy'), may hold values from 0 to 3
- support_mask: int32 [128, 64, 128], P('gx', 'gy'), may hold values from 1 to 255, as said below
Outputs:
- basis: float32 [8, 128, 64, 128], P(None, 'gx', 'gy')
- coarse_operator: float32 [27, 16, 16, 8], P(None, 'gx')
Inputs may be any that keep to these rules, and one draw needn't show every extreme that they name: `support_mask`: bit c = 4 a + 2 b + e of a cell's entry is set when the cell lies in the support of its channel-c node; the bit of the channel whose node is the cell's own 8 x 8 x 8 block is always set.
All inputs are finite; a program needn't handle non-finite values.
Results may differ from a plain program's by a relative error of at most 0.0001.
Values sent between devices are 32-bit elements; how exact they have to be, the bound alone decides.
A program may use at most 64 MiB of HBM per device.

v0:
```python
import jax
import jax.numpy as jnp
from jax import lax
from jax.sharding import PartitionSpec as P

ITERS = 2


OMEGA = 2.0 / 3.0
COARSE_SCALE = 1.0 / 64.0
HIGHEST = lax.Precision.HIGHEST


def extended(array, sides, width):
    for axis, dim in sides:
        count, length = (lax.axis_size(axis), array.shape[dim])
        up = [(i, (i + 1) % count) for i in range(count)]
        down = [(j, i) for i, j in up]
        last = lax.slice_in_dim(array, length - width, length, axis=dim)
        first = lax.slice_in_dim(array, 0, width, axis=dim)
        before = lax.ppermute(last, axis, up)
        after = lax.ppermute(first, axis, down)
        array = jnp.concatenate([before, array, after], axis=dim)
    return array


def conduct(classes):
    return jnp.where(
        classes == 0, 0.01, jnp.where(classes == 1, 0.1, jnp.where(classes == 2, 1.0, 10.0))
    ).astype(jnp.float32)


def harmonic(first, second):
    return 2.0 * first * second / (first + second)


def channel_bits(support):
    return jnp.stack([(support // 2**c % 2).astype(jnp.float32) for c in range(8)])


def axis_nodes(places, chosen):
    blocks = places // 8
    return jnp.where(
        blocks % 2 == chosen, blocks, jnp.where(places % 8 < 4, blocks - 1, blocks + 1)
    )


def weights(places, chosen):
    nodes = axis_nodes(places, chosen)
    return 1.0 - jnp.abs(places.astype(jnp.float32) - 8.0 * nodes.astype(jnp.float32) - 3.5) / 8.0


def normalize(fields):
    return fields / jnp.sum(fields, axis=0, keepdims=True)


def start_fields(bits, first_pos, second_pos, third_pos):
    listed = []
    for c in range(8):
        along_first = weights(first_pos, c // 4)
        along_second = weights(second_pos, c // 2 % 2)
        along_third = weights(third_pos, c % 2)
        listed.append(
            bits[c]
            * along_first[:, None, None]
            * along_second[None, :, None]
            * along_third[None, None, :]
        )
    return normalize(jnp.stack(listed))


def faces(padded_kappa):
    centre = padded_kappa[1:-1, 1:-1]
    west = harmonic(centre, padded_kappa[:-2, 1:-1])
    east = harmonic(centre, padded_kappa[2:, 1:-1])
    south = harmonic(centre, padded_kappa[1:-1, :-2])
    north = harmonic(centre, padded_kappa[1:-1, 2:])
    below = harmonic(centre, jnp.roll(centre, 1, 2))
    above = harmonic(centre, jnp.roll(centre, -1, 2))
    diag = west + east + south + north + below + above
    return ((west, east, south, north, below, above), diag)


def neighbours(padded, trans):
    west, east, south, north, below, above = trans
    centre = padded[:, 1:-1, 1:-1]
    near = (
        west * padded[:, :-2, 1:-1]
        + east * padded[:, 2:, 1:-1]
        + south * padded[:, 1:-1, :-2]
        + north * padded[:, 1:-1, 2:]
        + below * jnp.roll(centre, 1, 3)
        + above * jnp.roll(centre, -1, 3)
    )
    return (centre, near)


def smooth(padded, bits, trans, diag):
    centre, near = neighbours(padded, trans)
    return normalize(bits * ((1.0 - OMEGA) * centre + OMEGA * near / diag))


def apply_operator(padded, trans, diag):
    centre, near = neighbours(padded, trans)
    return diag * centre - near


def axis_table(places, base, rows, own_bit, other_bit):
    node_own = axis_nodes(places, own_bit)
    node_other = axis_nodes(places, other_bit)
    row_index = (node_own - base) % rows
    lines = (row_index[:, None] == jnp.arange(rows, dtype=jnp.int32)[None, :]).astype(jnp.float32)
    offset = (
        (node_other - node_own + 1)[:, None] == jnp.arange(3, dtype=jnp.int32)[None, :]
    ).astype(jnp.float32)
    return (lines[:, :, None] * offset[:, None, :]).reshape(places.shape[0], rows * 3)


def bit_tables(places, base, rows):
    return [
        jnp.stack([axis_table(places, base, rows, own_bit, other_bit) for other_bit in (0, 1)])
        for own_bit in (0, 1)
    ]


def coarse_terms(
    basis,
    images,
    first_pos,
    first_base,
    first_rows,
    second_pos,
    second_base,
    second_rows,
    third_pos,
    third_rows,
):
    tables_first = bit_tables(first_pos, first_base, first_rows)
    tables_second = bit_tables(second_pos, second_base, second_rows)
    tables_third = bit_tables(third_pos, 0, third_rows)
    chans, sx, sy, sz = images.shape
    grouped = images.reshape(2, 2, 2, sx, sy, sz)
    total = jnp.zeros((first_rows * 3, third_rows * 3, second_rows * 3), jnp.float32)
    for c in range(8):
        product = basis[c][None, None, None] * grouped
        section_one = jnp.einsum(
            "abexyz,ezk->abxyk", product, tables_third[c & 1], precision=HIGHEST
        )
        section_two = jnp.einsum(
            "abxyk,axi->biyk", section_one, tables_first[c >> 2 & 1], precision=HIGHEST
        )
        total = total + jnp.einsum(
            "biyk,byj->ikj", section_two, tables_second[c >> 1 & 1], precision=HIGHEST
        )
    arranged = total.reshape(first_rows, 3, third_rows, 3, second_rows, 3).transpose(
        1, 5, 3, 0, 2, 4
    )
    return arranged.reshape(27, first_rows, third_rows, second_rows)


def fold_edges(padded, dim):
    length = padded.shape[dim]
    inner = lax.slice_in_dim(padded, 2, length - 2, axis=dim)
    lower = lax.slice_in_dim(padded, 0, 1, axis=dim)
    upper = lax.slice_in_dim(padded, length - 1, length, axis=dim)
    return inner + lower + upper


def shards(classes, support_mask):
    width_first, width_second, depth = classes.shape
    start_first = lax.axis_index("gx") * width_first
    start_second = lax.axis_index("gy") * width_second
    third_pos = jnp.arange(depth, dtype=jnp.int32)
    padded_classes = extended(classes, (("gx", 0), ("gy", 1)), 1)
    trans, diag = faces(conduct(padded_classes))
    bits = channel_bits(support_mask)
    first_pos = start_first + jnp.arange(width_first, dtype=jnp.int32)
    second_pos = start_second + jnp.arange(width_second, dtype=jnp.int32)
    fields = start_fields(bits, first_pos, second_pos, third_pos)
    for step in range(ITERS + 1):
        padded = extended(fields, (("gx", 1), ("gy", 2)), 1)
        if step < ITERS:
            fields = smooth(padded, bits, trans, diag)
        else:
            images = apply_operator(padded, trans, diag)
    owned_first = start_first + jnp.arange(width_first, dtype=jnp.int32)
    owned_second = start_second + jnp.arange(width_second, dtype=jnp.int32)
    rows_first = width_first // 8 + 2
    base_first = start_first // 8 - 1
    rows_third = depth // 8
    rows_second = width_second * lax.axis_size("gy") // 8
    partial_terms = coarse_terms(
        fields,
        images,
        owned_first,
        base_first,
        rows_first,
        owned_second,
        0,
        rows_second,
        third_pos,
        rows_third,
    )
    summed = lax.psum(partial_terms, "gy")
    padded_rows = extended(summed, (("gx", 1),), 1)
    coarse = fold_edges(padded_rows, 1)
    return (fields, coarse * COARSE_SCALE)


def solution(mesh):
    in_specs = (P("gx", "gy", None), P("gx", "gy", None))
    out_specs = (P(None, "gx", "gy", None), P(None, "gx", None, None))
    return jax.shard_map(shards, mesh=mesh, in_specs=in_specs, out_specs=out_specs, check_vma=False)
```

profile of v0, /device:TPU:0, one launch (start us, length us, event | category | flops | bytes accessed | tf_op | source)
XLA Modules:
  0.0 124.6 jit_solution(1618516937053527967)
XLA Ops:
  0.7 1.0 bitcast_dynamic-update-slice_fusion.7
  1.7 1.0 bitcast_dynamic-update-slice_fusion.6
  2.8 1.0 bitcast_dynamic-update-slice_fusion.5
  3.8 1.0 bitcast_dynamic-update-slice_fusion.4
  4.9 1.8 %add_add_fusion.1 = f32[8,32,128]{2,1,0:T(8,128)S(1)} fusion(f32[8]{0:T(128)S(1)} %get-tuple-element.85, f32[32]{0:T(128)S(1)} %get-tuple-element.91, f32[128]{0:T(128)S(1)} %get-tuple-element.94, f32[128]{0:T(128)S(1)} %get-tuple-element.93, f32[32]{0:T(128)S(1)} %get-tuple-element.92, f32[8]{0:T(128)S(1)} %get-tuple-element.86, s32[8,32,128]{2,1,0:T(8,128)} %param.3), kind=kLoop, calls=%fused_computation.240 | loop fusion | flops 6389760 | bytes 263488 | tf_op jit(solution)/shard_map/reduce_sum | solution.py:54
  6.7 1.0 bitcast_dynamic-update-slice_fusion.3
  7.7 1.1 bitcast_dynamic-update-slice_fusion.2
  9.5 0.7 fusion.192
  10.3 2.9 %collective-permute-start.4 = (f32[8,1,32,128]{3,2,1,0:T(8,128)}, f32[8,1,32,128]{3,2,1,0:T(8,128)S(1)}, u32[]{:S(2)}, u32[]{:S(2)}) collective-permute-start(f32[8,1,32,128]{3,2,1,0:T(8,128)} %get-tuple-element.41), channel_id=1, source_target_pairs={{0,2},{2,4},{4,6},{6,8},{8,10},{10,12},{12,14},{14,16},{16,18},{18... | collective-permute-start | bytes 393224 | tf_op jit(solution)/shard_map/ppermute | solution.py:21
  13.2 4.0 %collective-permute-start.5 = (f32[8,1,32,128]{3,2,1,0:T(8,128)}, f32[8,1,32,128]{3,2,1,0:T(8,128)}, u32[]{:S(2)}, u32[]{:S(2)}) collective-permute-start(f32[8,1,32,128]{3,2,1,0:T(8,128)} %get-tuple-element.42), channel_id=1, source_target_pairs={{2,0},{4,2},{6,4},{8,6},{10,8},{12,10},{14,12},{16,14},{18,16},{20... | collective-permute-start | bytes 393224 | tf_op jit(solution)/shard_map/ppermute | solution.py:22
  17.8 5.6 %collective-permute-start.1 = (s32[1,32,128]{2,1,0:T(8,128)}, s32[1,32,128]{2,1,0:T(8,128)}, u32[]{:S(2)}, u32[]{:S(2)}) collective-permute-start(s32[1,32,128]{2,1,0:T(8,128)} %get-tuple-element.61), channel_id=1, source_target_pairs={{2,0},{4,2},{6,4},{8,6},{10,8},{12,10},{14,12},{16,14},{18,16},{20... | collective-permute-start | bytes 49160 | tf_op jit(solution)/shard_map/ppermute | solution.py:22
  23.4 1.3 %fusion.193 = (f32[8,8,32,1]{3,2,1,0:T(8,128)S(1)}, f32[8,8,32,1]{3,2,1,0:T(8,128)}) fusion(f32[8,8,32,128]{3,2,1,0:T(8,128)S(1)} %broadcast_divide_fusion.2), kind=kLoop, calls=%fused_computation.428 | loop fusion | bytes 32768 | tf_op jit(solution)/shard_map/jit(_roll_static)/slice | solution.py:92
  24.8 1.7 %fusion.194 = (f32[8,8,32,127]{3,2,1,0:T(8,128)}, f32[8,8,32,127]{3,2,1,0:T(8,128)}) fusion(f32[8,8,32,128]{3,2,1,0:T(8,128)S(1)} %broadcast_divide_fusion.2), kind=kLoop, calls=%fused_computation.429 | loop fusion | bytes 4161536 | tf_op jit(solution)/shard_map/jit(_roll_static)/slice | solution.py:92
  31.3 0.7 fusion.130
  35.1 1.2 fusion.134
  36.3 0.7 fusion.131
  37.6 0.7 fusion.132
  41.3 0.9 fusion.200
  42.2 0.8 fusion.201
  43.0 1.2 fusion.140
  44.2 1.3 %mul.855 = f32[8,3,3]{0,2,1:T(4,128)} broadcast(f32[8,3]{0,1:T(4,128)} %fusion.133), dimensions={0,1} | broadcast | bytes 384 | tf_op jit(solution)/shard_map/mul | solution.py:116
  45.5 1.3 %mul.856 = f32[1,8,9]{1,2,0:T(8,128)} reshape(f32[8,3,3]{0,2,1:T(4,128)} %mul.855) | data formatting | bytes 576 | tf_op jit(solution)/shard_map/mul | solution.py:116
  46.8 1.3 %mul.913 = f32[8,3,3]{0,2,1:T(4,128)} broadcast(f32[8,3]{0,1:T(4,128)} %fusion.139), dimensions={0,1} | broadcast | bytes 384 | tf_op jit(solution)/shard_map/mul | solution.py:116
  48.1 1.3 %mul.914 = f32[1,8,9]{1,2,0:T(8,128)} reshape(f32[8,3,3]{0,2,1:T(4,128)} %mul.913) | data formatting | bytes 576 | tf_op jit(solution)/shard_map/mul | solution.py:116
  49.4 1.3 %mul.861 = f32[8,3,3]{0,2,1:T(4,128)} broadcast(f32[8,3]{0,1:T(4,128)} %fusion.134), dimensions={0,2} | broadcast | bytes 384 | tf_op jit(solution)/shard_map/mul | solution.py:116
  50.6 1.3 %mul.862 = f32[1,8,9]{1,2,0:T(8,128)} reshape(f32[8,3,3]{0,2,1:T(4,128)} %mul.861) | data formatting | bytes 576 | tf_op jit(solution)/shard_map/mul | solution.py:116
  51.9 1.2 mul.915
  53.2 1.3 %mul.916 = f32[1,8,9]{1,2,0:T(8,128)} reshape(f32[8,3,3]{0,2,1:T(4,128)} %mul.915) | data formatting | bytes 576 | tf_op jit(solution)/shard_map/mul | solution.py:116
  54.5 1.2 mul.857
  55.6 1.3 %mul.858 = f32[9]{0:T(128)} reshape(f32[3,3]{1,0:T(4,128)} %mul.857) | data formatting | bytes 72 | tf_op jit(solution)/shard_map/mul | solution.py:116
  56.9 0.7 constant_dynamic-update-slice_fusion.2
  57.6 0.7 constant_dynamic-update-slice_fusion
  59.0 0.8 fusion.202
  60.1 1.0 pad_maximum_fusion.36
  62.7 2.5 %fusion.184 = (f32[8,32,128]{2,1,0:T(8,128)S(1)}, f32[8,8,32,128]{3,2,1,0:T(8,128)S(1)}) fusion(f32[8,8,32,128]{3,2,1,0:T(8,128)S(1)} %bitcast_dynamic-update-slice_fusion.8, f32[8,32,128]{2,1,0:T(8,128)S(1)} %get-tuple-element.8, f32[8,8,32,1]{3,2,1,0:T(8,128)S(1)} %copy-done.2, f32[8,8,32,127]{3,2,1,0:T(8,128)S(1)} %copy-done.4, ...), kind=kLoop, calls=%fused_computation.420 | loop fusion | flops 7045120 | bytes 6635520 | tf_op jit(solution)/shard_map/reduce_sum | solution.py:54
  65.5 5.6 %collective-permute-start.9 = (f32[8,1,32,128]{3,2,1,0:T(8,128)S(1)}, f32[8,1,32,128]{3,2,1,0:T(8,128)S(1)}, u32[]{:S(2)}, u32[]{:S(2)}) collective-permute-start(f32[8,1,32,128]{3,2,1,0:T(8,128)S(1)} %get-tuple-element.36), channel_id=1, source_target_pairs={{2,0},{4,2},{6,4},{8,6},{10,8},{12,10},{14,12},{16,14},{18,16},{20... | collective-permute-start | bytes 393224 | tf_op jit(solution)/shard_map/ppermute | solution.py:22
  71.5 3.2 %collective-permute-done.8 = f32[8,1,32,128]{3,2,1,0:T(8,128)S(1)} collective-permute-done((f32[8,1,32,128]{3,2,1,0:T(8,128)S(1)}, f32[8,1,32,128]{3,2,1,0:T(8,128)S(1)}, u32[]{:S(2)}, u32[]{:S(2)}) %collective-permute-start.8) | collective-permute-done | bytes 131104 | tf_op jit(solution)/shard_map/ppermute | solution.py:21
  76.2 1.6 %fusion.182 = (f32[8,32,128]{2,1,0:T(8,128)S(1)}, f32[8,8,32,128]{3,2,1,0:T(8,128)S(1)}) fusion(f32[8,8,32,128]{3,2,1,0:T(8,128)S(1)} %bitcast_dynamic-update-slice_fusion.8, f32[8,32,128]{2,1,0:T(8,128)S(1)} %get-tuple-element.8, f32[8,8,32,1]{3,2,1,0:T(8,128)S(1)} %get-tuple-element.38, f32[8,8,32,127]{3,2,1,0:T(8,128)S(1)} %get-tuple-element.40, ...), kind=kLoop, calls=%fused_computation.419 | loop fusion | flops 7045120 | bytes 6635520 | tf_op jit(solution)/shard_map/reduce_sum | solution.py:54
  78.5 5.6 %collective-permute-start.13 = (f32[8,1,32,128]{3,2,1,0:T(8,128)S(1)}, f32[8,1,32,128]{3,2,1,0:T(8,128)S(1)}, u32[]{:S(2)}, u32[]{:S(2)}) collective-permute-start(f32[8,1,32,128]{3,2,1,0:T(8,128)S(1)} %get-tuple-element.34), channel_id=1, source_target_pairs={{2,0},{4,2},{6,4},{8,6},{10,8},{12,10},{14,12},{16,14},{18,16},{20... | collective-permute-start | bytes 393224 | tf_op jit(solution)/shard_map/ppermute | solution.py:22
  84.5 3.3 %collective-permute-done.12 = f32[8,1,32,128]{3,2,1,0:T(8,128)S(1)} collective-permute-done((f32[8,1,32,128]{3,2,1,0:T(8,128)S(1)}, f32[8,1,32,128]{3,2,1,0:T(8,128)S(1)}, u32[]{:S(2)}, u32[]{:S(2)}) %collective-permute-start.12) | collective-permute-done | bytes 131104 | tf_op jit(solution)/shard_map/ppermute | solution.py:21
  88.5 0.6 collective-permute-done.14
  89.3 1.1 fusion.11
  90.4 1.0 convolution_bitcast_fusion.7
  91.4 0.8 fusion.65
  92.2 1.0 convolution_bitcast_fusion.6
  93.2 0.8 fusion.63
  94.1 1.0 convolution_bitcast_fusion.5
  95.0 0.8 fusion.61
  95.9 1.0 convolution_bitcast_fusion.4
  96.9 0.8 fusion.59
  98.4 1.0 convolution_bitcast_fusion.3
  99.8 0.8 fusion.57
  101.2 1.0 convolution_bitcast_fusion.2
  102.2 0.8 fusion.55
  103.4 1.0 convolution_bitcast_fusion.1
  104.4 0.8 fusion.53
  105.6 1.0 convolution_bitcast_fusion
  106.5 0.8 fusion.51
  108.1 0.9 reshape.1069
  109.1 1.4 %copy.5 = f32[3,3,3,3,16,8]{4,5,3,2,1,0:T(8,128)S(1)} copy(f32[3,3,3,3,16,8]{2,4,1,5,0,3:T(8,128)S(1)} %bitcast.263) | data formatting | bytes 82944 | tf_op jit(solution)/shard_map/transpose | solution.py:155
  110.4 4.3 %psum.7 = f32[27,3,16,8]{2,3,1,0:T(8,128)S(1)} all-reduce(f32[27,3,16,8]{2,3,1,0:T(8,128)S(1)} %bitcast.264), channel_id=1, replica_groups=mesh['gx'=16,'gy'=2] {'gy'}, use_global_device_ids=true, to_apply=%region_2.3 | all-reduce | flops 10368 | bytes 82944 | tf_op jit(solution)/shard_map/psum | solution.py:204
  114.8 5.6 %collective-permute-start.17 = (f32[27,1,16,8]{2,3,1,0:T(8,128)S(1)}, f32[27,1,16,8]{2,3,1,0:T(8,128)S(1)}, u32[]{:S(2)}, u32[]{:S(2)}) collective-permute-start(f32[27,1,16,8]{2,3,1,0:T(8,128)S(1)} %get-tuple-element.48), channel_id=1, source_target_pairs={{2,0},{4,2},{6,4},{8,6},{10,8},{12,10},{14,12},{16,14},{18,16},{20... | collective-permute-start | bytes 41480 | tf_op jit(solution)/shard_map/ppermute | solution.py:22
  120.5 3.3 %collective-permute-done.16 = f32[27,1,16,8]{2,3,1,0:T(8,128)S(1)} collective-permute-done((f32[27,1,16,8]{2,3,1,0:T(8,128)S(1)}, f32[27,1,16,8]{2,3,1,0:T(8,128)S(1)}, u32[]{:S(2)}, u32[]{:S(2)}) %collective-permute-start.16) | collective-permute-done | bytes 13856 | tf_op jit(solution)/shard_map/ppermute | solution.py:21
  123.8 0.8 copy.6
  (115 shorter events, 22.6 us)
Async XLA Ops:
  0.6 8.2 %copy-start.1 = (s32[8,32,128]{2,1,0:T(8,128)S(1)}, s32[8,32,128]{2,1,0:T(8,128)}, u32[]{:S(2)}) copy-start(s32[8,32,128]{2,1,0:T(8,128)} %param.3) | copy-start | bytes 393220
  8.8 8.4 %copy-start.5 = (s32[8,32,128]{2,1,0:T(8,128)S(1)}, s32[8,32,128]{2,1,0:T(8,128)}, u32[]{:S(2)}) copy-start(s32[8,32,128]{2,1,0:T(8,128)} %param.2) | copy-start | bytes 393220
  10.3 49.8 %collective-permute-start.4 = (f32[8,1,32,128]{3,2,1,0:T(8,128)}, f32[8,1,32,128]{3,2,1,0:T(8,128)S(1)}, u32[]{:S(2)}, u32[]{:S(2)}) collective-permute-start(f32[8,1,32,128]{3,2,1,0:T(8,128)} %get-tuple-element.41), channel_id=1, source_target_pairs={{0,2},{2,4},{4,6},{6,8},{8,10},{10,12},{12,14},{14,16},{16,18},{18... | collective-permute-start | bytes 393224 | tf_op jit(solution)/shard_map/ppermute | solution.py:21
  13.2 46.9 %collective-permute-start.5 = (f32[8,1,32,128]{3,2,1,0:T(8,128)}, f32[8,1,32,128]{3,2,1,0:T(8,128)}, u32[]{:S(2)}, u32[]{:S(2)}) collective-permute-start(f32[8,1,32,128]{3,2,1,0:T(8,128)} %get-tuple-element.42), channel_id=1, source_target_pairs={{2,0},{4,2},{6,4},{8,6},{10,8},{12,10},{14,12},{16,14},{18,16},{20... | collective-permute-start | bytes 393224 | tf_op jit(solution)/shard_map/ppermute | solution.py:22
  17.8 39.1 %collective-permute-start = (s32[1,32,128]{2,1,0:T(8,128)}, s32[1,32,128]{2,1,0:T(8,128)}, u32[]{:S(2)}, u32[]{:S(2)}) collective-permute-start(s32[1,32,128]{2,1,0:T(8,128)} %get-tuple-element.62), channel_id=1, source_target_pairs={{0,2},{2,4},{4,6},{6,8},{8,10},{10,12},{12,14},{14,16},{16,18},{18... | collective-permute-start | bytes 49160 | tf_op jit(solution)/shard_map/ppermute | solution.py:21
  17.8 39.8 %collective-permute-start.1 = (s32[1,32,128]{2,1,0:T(8,128)}, s32[1,32,128]{2,1,0:T(8,128)}, u32[]{:S(2)}, u32[]{:S(2)}) collective-permute-start(s32[1,32,128]{2,1,0:T(8,128)} %get-tuple-element.61), channel_id=1, source_target_pairs={{2,0},{4,2},{6,4},{8,6},{10,8},{12,10},{14,12},{16,14},{18,16},{20... | collective-permute-start | bytes 49160 | tf_op jit(solution)/shard_map/ppermute | solution.py:22
  26.5 14.2 %copy-start.6 = (f32[3]{0:T(128)}, f32[3]{0:T(128)S(1)}, u32[]{:S(2)}) copy-start(f32[3]{0:T(128)S(1)} %compare_convert_fusion) | copy-start | bytes 40
  58.4 1.4 %collective-permute-start.2 = (s32[10,1,128]{2,1,0:T(1,128)S(1)}, s32[10,1,128]{2,1,0:T(1,128)S(1)}, u32[]{:S(2)}, u32[]{:S(2)}) collective-permute-start(s32[10,1,128]{2,1,0:T(1,128)S(1)} %get-tuple-element.53), channel_id=1, source_target_pairs={{0,1},{1,0},{2,3},{3,2},{4,5},{5,4},{6,7},{7,6},{8,9},{9,8},{10,11... | collective-permute-start | bytes 15368 | tf_op jit(solution)/shard_map/ppermute | solution.py:21
  58.5 1.3 %collective-permute-start.3 = (s32[10,1,128]{2,1,0:T(1,128)S(1)}, s32[10,1,128]{2,1,0:T(1,128)S(1)}, u32[]{:S(2)}, u32[]{:S(2)}) collective-permute-start(s32[10,1,128]{2,1,0:T(1,128)S(1)} %get-tuple-element.54), channel_id=1, source_target_pairs={{1,0},{0,1},{3,2},{2,3},{5,4},{4,5},{7,6},{6,7},{9,8},{8,9},{11,10... | collective-permute-start | bytes 15368 | tf_op jit(solution)/shard_map/ppermute | solution.py:22
  60.1 2.7 %copy-start.2 = (f32[8,8,32,1]{3,2,1,0:T(8,128)S(1)}, f32[8,8,32,1]{3,2,1,0:T(8,128)}, u32[]{:S(2)}) copy-start(f32[8,8,32,1]{3,2,1,0:T(8,128)} %get-tuple-element.44) | copy-start | bytes 24580
  60.1 2.7 %copy-start.3 = (f32[8,8,32,127]{3,2,1,0:T(8,128)S(1)}, f32[8,8,32,127]{3,2,1,0:T(8,128)}, u32[]{:S(2)}) copy-start(f32[8,8,32,127]{3,2,1,0:T(8,128)} %get-tuple-element.45) | copy-start | bytes 3121156
  60.1 2.6 %copy-start.4 = (f32[8,8,32,127]{3,2,1,0:T(8,128)S(1)}, f32[8,8,32,127]{3,2,1,0:T(8,128)}, u32[]{:S(2)}) copy-start(f32[8,8,32,127]{3,2,1,0:T(8,128)} %get-tuple-element.46) | copy-start | bytes 3121156
  61.1 1.3 %collective-permute-start.6 = (f32[8,10,1,128]{3,2,1,0:T(1,128)S(1)}, f32[8,10,1,128]{3,2,1,0:T(1,128)S(1)}, u32[]{:S(2)}, u32[]{:S(2)}) collective-permute-start(f32[8,10,1,128]{3,2,1,0:T(1,128)S(1)} %get-tuple-element.19), channel_id=1, source_target_pairs={{0,1},{1,0},{2,3},{3,2},{4,5},{5,4},{6,7},{7,6},{8,9},{9,8},{10,11... | collective-permute-start | bytes 122888 | tf_op jit(solution)/shard_map/ppermute | solution.py:21
  61.5 1.2 collective-permute-start.7
  65.4 9.2 %collective-permute-start.8 = (f32[8,1,32,128]{3,2,1,0:T(8,128)S(1)}, f32[8,1,32,128]{3,2,1,0:T(8,128)S(1)}, u32[]{:S(2)}, u32[]{:S(2)}) collective-permute-start(f32[8,1,32,128]{3,2,1,0:T(8,128)S(1)} %get-tuple-element.35), channel_id=1, source_target_pairs={{0,2},{2,4},{4,6},{6,8},{8,10},{10,12},{12,14},{14,16},{16,18},{18... | collective-permute-start | bytes 393224 | tf_op jit(solution)/shard_map/ppermute | solution.py:21
  65.5 9.2 %collective-permute-start.9 = (f32[8,1,32,128]{3,2,1,0:T(8,128)S(1)}, f32[8,1,32,128]{3,2,1,0:T(8,128)S(1)}, u32[]{:S(2)}, u32[]{:S(2)}) collective-permute-start(f32[8,1,32,128]{3,2,1,0:T(8,128)S(1)} %get-tuple-element.36), channel_id=1, source_target_pairs={{2,0},{4,2},{6,4},{8,6},{10,8},{12,10},{14,12},{16,14},{18,16},{20... | collective-permute-start | bytes 393224 | tf_op jit(solution)/shard_map/ppermute | solution.py:22
  74.7 1.3 %collective-permute-start.10 = (f32[8,10,1,128]{3,2,1,0:T(1,128)S(1)}, f32[8,10,1,128]{3,2,1,0:T(1,128)S(1)}, u32[]{:S(2)}, u32[]{:S(2)}) collective-permute-start(f32[8,10,1,128]{3,2,1,0:T(1,128)S(1)} %get-tuple-element.17), channel_id=1, source_target_pairs={{0,1},{1,0},{2,3},{3,2},{4,5},{5,4},{6,7},{7,6},{8,9},{9,8},{10,11... | collective-permute-start | bytes 122888 | tf_op jit(solution)/shard_map/ppermute | solution.py:21
  74.8 1.4 %collective-permute-start.11 = (f32[8,10,1,128]{3,2,1,0:T(1,128)S(1)}, f32[8,10,1,128]{3,2,1,0:T(1,128)S(1)}, u32[]{:S(2)}, u32[]{:S(2)}) collective-permute-start(f32[8,10,1,128]{3,2,1,0:T(1,128)S(1)} %get-tuple-element.18), channel_id=1, source_target_pairs={{1,0},{0,1},{3,2},{2,3},{5,4},{4,5},{7,6},{6,7},{9,8},{8,9},{11,10... | collective-permute-start | bytes 122888 | tf_op jit(solution)/shard_map/ppermute | solution.py:22
  78.0 11.3 %copy-start = (f32[8,8,32,128]{3,2,1,0:T(8,128)}, f32[8,8,32,128]{3,2,1,0:T(8,128)S(1)}, u32[]{:S(2)}) copy-start(f32[8,8,32,128]{3,2,1,0:T(8,128)S(1)} %broadcast_divide_fusion) | copy-start | bytes 3145732
  78.4 9.4 %collective-permute-start.12 = (f32[8,1,32,128]{3,2,1,0:T(8,128)S(1)}, f32[8,1,32,128]{3,2,1,0:T(8,128)S(1)}, u32[]{:S(2)}, u32[]{:S(2)}) collective-permute-start(f32[8,1,32,128]{3,2,1,0:T(8,128)S(1)} %get-tuple-element.33), channel_id=1, source_target_pairs={{0,2},{2,4},{4,6},{6,8},{8,10},{10,12},{12,14},{14,16},{16,18},{18... | collective-permute-start | bytes 393224 | tf_op jit(solution)/shard_map/ppermute | solution.py:21
  78.5 9.3 %collective-permute-start.13 = (f32[8,1,32,128]{3,2,1,0:T(8,128)S(1)}, f32[8,1,32,128]{3,2,1,0:T(8,128)S(1)}, u32[]{:S(2)}, u32[]{:S(2)}) collective-permute-start(f32[8,1,32,128]{3,2,1,0:T(8,128)S(1)} %get-tuple-element.34), channel_id=1, source_target_pairs={{2,0},{4,2},{6,4},{8,6},{10,8},{12,10},{14,12},{16,14},{18,16},{20... | collective-permute-start | bytes 393224 | tf_op jit(solution)/shard_map/ppermute | solution.py:22
  87.9 1.3 %collective-permute-start.14 = (f32[8,10,1,128]{3,2,1,0:T(1,128)S(1)}, f32[8,10,1,128]{3,2,1,0:T(1,128)S(1)}, u32[]{:S(2)}, u32[]{:S(2)}) collective-permute-start(f32[8,10,1,128]{3,2,1,0:T(1,128)S(1)} %get-tuple-element.15), channel_id=1, source_target_pairs={{0,1},{1,0},{2,3},{3,2},{4,5},{5,4},{6,7},{7,6},{8,9},{9,8},{10,11... | collective-permute-start | bytes 122888 | tf_op jit(solution)/shard_map/ppermute | solution.py:21
  88.0 1.4 %collective-permute-start.15 = (f32[8,10,1,128]{3,2,1,0:T(1,128)S(1)}, f32[8,10,1,128]{3,2,1,0:T(1,128)S(1)}, u32[]{:S(2)}, u32[]{:S(2)}) collective-permute-start(f32[8,10,1,128]{3,2,1,0:T(1,128)S(1)} %get-tuple-element.16), channel_id=1, source_target_pairs={{1,0},{0,1},{3,2},{2,3},{5,4},{4,5},{7,6},{6,7},{9,8},{8,9},{11,10... | collective-permute-start | bytes 122888 | tf_op jit(solution)/shard_map/ppermute | solution.py:22
  114.8 9.0 %collective-permute-start.16 = (f32[27,1,16,8]{2,3,1,0:T(8,128)S(1)}, f32[27,1,16,8]{2,3,1,0:T(8,128)S(1)}, u32[]{:S(2)}, u32[]{:S(2)}) collective-permute-start(f32[27,1,16,8]{2,3,1,0:T(8,128)S(1)} %get-tuple-element.47), channel_id=1, source_target_pairs={{0,2},{2,4},{4,6},{6,8},{8,10},{10,12},{12,14},{14,16},{16,18},{18... | collective-permute-start | bytes 41480 | tf_op jit(solution)/shard_map/ppermute | solution.py:21
  114.8 9.0 %collective-permute-start.17 = (f32[27,1,16,8]{2,3,1,0:T(8,128)S(1)}, f32[27,1,16,8]{2,3,1,0:T(8,128)S(1)}, u32[]{:S(2)}, u32[]{:S(2)}) collective-permute-start(f32[27,1,16,8]{2,3,1,0:T(8,128)S(1)} %get-tuple-element.48), channel_id=1, source_target_pairs={{2,0},{4,2},{6,4},{8,6},{10,8},{12,10},{14,12},{16,14},{18,16},{20... | collective-permute-start | bytes 41480 | tf_op jit(solution)/shard_map/ppermute | solution.py:22
where the time goes:
time: 126 us; the launch traced here: 125 us
  starting transfers between devices  31.9 us (25%)
  local copies, waits for them, and re-layouts  29.1 us (23%)
  other arithmetic  28.6 us (23%)
  matrix products  17.6 us (14%)
  waiting for transfers between devices  12 us (10%)
  blocking collectives  4.3 us (3%)
    ppermute x9, starting transfers between devices, extended(): after = lax.ppermute(first, axis, down)  28.1 us
    mul x30, local copies, waits for them, and re-layouts, axis_table(): lines[:, :, None] * offset[:, None, :]  18.3 us
    ppermute x9, waiting for transfers between devices, extended(): before = lax.ppermute(last, axis, up)  11.3 us
    dot_general x8, matrix products, coarse_terms(): jnp.einsum('abexyz,ezk->abxyk', product, tables_third[c & 1], precision=H...  7.78 us
    unnamed x11, other arithmetic  7.06 us
    dot_general x8, matrix products, coarse_terms(): jnp.einsum('abxyk,axi->biyk', section_one, tables_first[c >> 2 & 1], prec...  6.66 us
    reduce_sum x3, other arithmetic, normalize(): return fields / jnp.sum(fields, axis=0, keepdims=True)  5.97 us
    psum x1, blocking collectives, shards(): summed = lax.psum(partial_terms, 'gy')  4.3 us
  transfers between devices with their start and end apart: 18, of which 9 were waited for; matrix products, arithmetic and copies ran while one was open for 30% of the time, Pallas kernels for 0%

commit v1 on v0

v1 whole, which is shorter than its diff:
```python
import functools

import jax
import jax.numpy as jnp
from jax import lax
from jax.experimental import pallas as pl
from jax.experimental.pallas import tpu as pltpu
from jax.sharding import PartitionSpec as P

COARSE_SCALE = 1.0 / 64.0
HALO = 3
EDGE = 8
MESH = pl.DeviceIdType.MESH


def node_of(places, chosen):
    blocks = places >> 3
    same = (blocks & 1) == chosen
    return jnp.where(same, blocks, jnp.where((places & 7) < 4, blocks - 1, blocks + 1))


def weight_of(places, chosen):
    distance = (places - 8 * node_of(places, chosen)).astype(jnp.float32) - 3.5
    return 1.0 - jnp.abs(distance) / 8.0


def harmonic(first, second):
    return 2.0 * first * second / (first + second)


def split_dot(left, right, left_is_table):
    data = right if left_is_table else left
    high = data.astype(jnp.bfloat16)
    low = (data - high.astype(jnp.float32)).astype(jnp.bfloat16)
    if left_is_table:
        return jnp.dot(left, high, preferred_element_type=jnp.float32) + jnp.dot(
            left, low, preferred_element_type=jnp.float32
        )
    return jnp.dot(high, right, preferred_element_type=jnp.float32) + jnp.dot(
        low, right, preferred_element_type=jnp.float32
    )


def kernel(
    nx,
    ny,
    cls_hbm,
    msk_hbm,
    basis_hbm,
    coarse_ref,
    cells,
    edge,
    sides,
    kappa,
    t_east,
    t_north,
    t_above,
    diag,
    plane_w,
    phi_a,
    phi_b,
    image,
    pairs,
    table_y,
    table_z,
    terms,
    to_low,
    to_high,
    to_own,
    from_low,
    from_high,
    from_own,
    load_sem,
    halo_send,
    halo_recv,
    term_send,
    term_recv,
    out_sem,
):
    width, rows, depth = cls_hbm.shape
    wide = rows + EDGE
    count_y = rows * ny // 8
    count_z = depth // 8
    gx, gy = lax.axis_index("gx"), lax.axis_index("gy")
    parity = lax.rem(gx, 2)
    own = pl.ds(HALO, width)
    main = pl.ds(0, rows)
    tail = pl.ds(rows, EDGE)

    def peer(dx, dy):
        return (lax.rem(gx + dx + nx, nx), lax.rem(gy + dy + ny, ny))

    loads = [
        pltpu.make_async_copy(ref, cells.at[i, own, main, :], load_sem.at[i])
        for i, ref in enumerate((cls_hbm, msk_hbm))
    ]
    for copy in loads:
        copy.start()

    partners = [(dx, dy) for dx in (-1, 0, 1) for dy in range(ny) if (dx, dy) != (0, 0)]
    barrier = pltpu.get_barrier_semaphore()
    for dx, dy in partners:
        pl.semaphore_signal(barrier, inc=1, device_id=peer(dx, dy), device_id_type=MESH)

    row_pos = lax.broadcasted_iota(jnp.int32, (wide, depth), 0)
    second = gy * rows + jnp.where(row_pos < rows + EDGE // 2, row_pos, row_pos - wide)
    third = lax.broadcasted_iota(jnp.int32, (wide, depth), 1)
    for b in (0, 1):
        for e in (0, 1):
            plane_w[2 * b + e] = weight_of(second, b) * weight_of(third, e)
    place = lax.broadcasted_iota(jnp.int32, (depth, 128), 0)
    lane = lax.broadcasted_iota(jnp.int32, (depth, 128), 1)
    for e in (0, 1):
        for other in (0, 1):
            mine = node_of(place, e)
            shift = node_of(place, other) - mine + 1
            column = lax.rem(mine + count_z, count_z) + count_z * shift
            table_z[pl.ds((2 * e + other) * depth, depth), :] = jnp.where(
                column == lane, 1.0, 0.0
            ).astype(jnp.bfloat16)
    line = lax.broadcasted_iota(jnp.int32, table_y.shape, 0)
    column = lax.broadcasted_iota(jnp.int32, table_y.shape, 1)
    bits = column // rows
    spot = gy * rows + column - rows * bits
    mine = jnp.where(bits >= 2, node_of(spot, 1), node_of(spot, 0))
    theirs = jnp.where((bits & 1) == 1, node_of(spot, 1), node_of(spot, 0))
    target = lax.rem(mine + count_y, count_y) + count_y * (theirs - mine + 1)
    table_y[...] = jnp.where(target == line, 1.0, 0.0).astype(jnp.bfloat16)

    for copy in loads:
        copy.wait()
    sub = lax.broadcasted_iota(jnp.int32, (width, EDGE, depth), 1)
    if ny == 2:
        for i in (0, 1):
            edge[i] = jnp.where(
                sub < EDGE // 2,
                cells[i, own, pl.ds(0, EDGE), :],
                cells[i, own, pl.ds(rows - EDGE, EDGE), :],
            )
    pl.semaphore_wait(barrier, len(partners))

    copies = {}

    def send(key, src, dst, dx, dy):
        index = len(copies)
        copies[key] = pltpu.make_async_remote_copy(
            src_ref=src,
            dst_ref=dst,
            send_sem=halo_send.at[index],
            recv_sem=halo_recv.at[index],
            device_id=peer(dx, dy),
            device_id_type=MESH,
        )
        copies[key].start()

    spans = {
        0: (0, HALO, width),
        -1: (0, HALO + width, HALO),
        1: (width - HALO, 0, HALO),
    }
    for dx in (1, -1):
        start, land, size = spans[dx]
        send(
            ("x", dx),
            cells.at[:, pl.ds(HALO + start, size), main, :],
            cells.at[:, pl.ds(land, size), main, :],
            dx,
            0,
        )
    for dx in (1, -1, 0):
        start, land, size = spans[dx]
        if dx == 0:
            land = HALO
        if ny == 2:
            send(
                ("y", dx, 0),
                edge.at[:, pl.ds(start, size), :, :],
                cells.at[:, pl.ds(land, size), tail, :],
                dx,
                1,
            )
        else:
            for side, dy, first in ((0, -1, 0), (1, 1, rows - EDGE)):
                send(
                    ("y", dx, side),
                    cells.at[:, pl.ds(HALO + start, size), pl.ds(first, EDGE), :],
                    sides.at[side, :, pl.ds(land, size), :, :],
                    dx,
                    dy,
                )

    def receive(dx):
        _, land, size = spans[dx]
        if dx == 0:
            land = HALO
        else:
            copies[("x", dx)].wait_recv()
        if ny == 2:
            copies[("y", dx, 0)].wait_recv()
        else:
            for side in (0, 1):
                copies[("y", dx, side)].wait_recv()
            part = lax.broadcasted_iota(jnp.int32, (size, EDGE, depth), 1)
            for i in (0, 1):
                cells[i, pl.ds(land, size), tail, :] = jnp.where(
                    part < EDGE // 2,
                    sides[0, i, pl.ds(land, size), :, :],
                    sides[1, i, pl.ds(land, size), :, :],
                )

    def up(plane, axis):
        return pltpu.roll(plane, 1, axis)

    def down(plane, axis):
        return pltpu.roll(plane, plane.shape[axis] - 1, axis)

    def prepare(x):
        classes = cells[0, x]
        mask = cells[1, x]
        k = jnp.where(
            classes == 0, 0.01, jnp.where(classes == 1, 0.1, jnp.where(classes == 2, 1.0, 10.0))
        ).astype(jnp.float32)
        kappa[x] = k
        t_north[x] = harmonic(k, down(k, 0))
        t_above[x] = harmonic(k, down(k, 1))
        at = jnp.full((1, depth), gx * width + x - HALO, jnp.int32)
        along = [weight_of(at, 0), weight_of(at, 1)]
        fields = []
        total = None
        for c in range(8):
            value = jnp.where((mask & (1 << c)) != 0, along[c // 4] * plane_w[c % 4], 0.0)
            fields.append(value)
            total = value if total is None else total + value
        scale = 1.0 / total
        for c in range(8):
            phi_a[c, x] = fields[c] * scale

    def join(x):
        t_east[x] = harmonic(kappa[x], kappa[x + 1])

    def gather(x):
        diag[x] = (
            t_east[x - 1]
            + t_east[x]
            + up(t_north[x], 0)
            + t_north[x]
            + up(t_above[x], 1)
            + t_above[x]
        )

    def near(source, c, x, coefs):
        west, east, south, north, below, above = coefs
        field = source[c, x]
        return field, (
            west * source[c, x - 1]
            + east * source[c, x + 1]
            + south * up(field, 0)
            + north * down(field, 0)
            + below * up(field, 1)
            + above * down(field, 1)
        )

    def coefficients(x):
        north, above = t_north[x], t_above[x]
        return (t_east[x - 1], t_east[x], up(north, 0), north, up(above, 1), above)

    def smooth(source, target, x):
        coefs = coefficients(x)
        half = 0.5 * diag[x]
        mask = cells[1, x]
        total = None
        for c in range(8):
            field, sums = near(source, c, x, coefs)
            value = jnp.where((mask & (1 << c)) != 0, half * field + sums, 0.0)
            target[c, x] = value
            total = value if total is None else total + value
        scale = 1.0 / total
        for c in range(8):
            target[c, x] = target[c, x] * scale

    def apply(source, x):
        coefs = coefficients(x)
        centre = diag[x]
        for d in range(8):
            field, sums = near(source, d, x, coefs)
            image[d, x - HALO] = (centre * field - sums)[:rows]

    def inner(work, first, last):
        def body(x, carry):
            work(x)
            return carry

        lax.fori_loop(first, last, body, 0)

    def outer(work, low, high, size=HALO):
        def body(i, carry):
            work(i + low + (i // size) * (high - low - size))
            return carry

        lax.fori_loop(0, 2 * size, body, 0)

    top = HALO + width
    receive(0)
    inner(prepare, HALO, top)
    inner(join, HALO, top - 1)
    inner(gather, HALO + 1, top - 1)
    inner(functools.partial(smooth, phi_a, phi_b), HALO + 1, top - 1)

    receive(1)
    receive(-1)
    outer(prepare, 0, top)
    outer(join, 0, top - 1)
    outer(gather, 1, top - 1)
    outer(functools.partial(smooth, phi_a, phi_b), 1, top - 1)
    inner(functools.partial(smooth, phi_b, phi_a), HALO - 1, top + 1)
    stored = pltpu.make_async_copy(phi_a.at[:, own, main, :], basis_hbm, out_sem)
    stored.start()
    inner(functools.partial(apply, phi_a), HALO, top)

    tiles = rows // 8

    def products(step, carry):
        half = step // tiles
        tile = pl.multiple_of(lax.rem(step, tiles) * 8, 8)
        at = pl.ds(tile, 8)
        for c_half in range(2):
            total = {}
            for i in range(width // 2):
                x = half * (width // 2) + i
                images = [image[d, x, at, :] for d in range(8)]
                for c in range(4 * c_half, 4 * c_half + 4):
                    field = phi_a[c, x + HALO, at, :]
                    for d in range(8):
                        value = field * images[d]
                        total[c, d] = value if i == 0 else total[c, d] + value
            for (c, d), value in total.items():
                group = ((c >> 2) * 2 + (d >> 2)) * 2 + half
                block = (c >> 1 & 1) * 2 + (d >> 1 & 1)
                column = (c & 1) * 2 + (d & 1)
                pairs[group, pl.ds(block * rows + tile, 8), pl.ds(column * depth, depth)] = value
        return carry

    lax.fori_loop(0, 2 * tiles, products, 0)

    for group in range(8):
        section = split_dot(pairs[group], table_z[...], False)
        terms[group] = split_dot(table_y[...], section, True)

    def term(a, other, half):
        return terms[(a * 2 + other) * 2 + half]

    mine, off = parity, 1 - parity
    to_low[0] = term(off, off, 0)
    to_low[1] = term(off, mine, 0)
    to_high[0] = term(off, off, 1)
    to_high[1] = term(off, mine, 1)
    to_own[0] = term(mine, off, 0)
    to_own[1] = term(mine, mine, 0) + term(mine, mine, 1)
    to_own[2] = term(mine, off, 1)

    sent = []
    for source, landing, dx in ((to_low, from_high, -1), (to_high, from_low, 1), (to_own, from_own, 0)):
        for dy in range(ny):
            if (dx, dy) == (0, 0):
                continue
            index = len(sent)
            copy = pltpu.make_async_remote_copy(
                src_ref=source,
                dst_ref=landing.at[dy],
                send_sem=term_send.at[index],
                recv_sem=term_recv.at[index],
                device_id=peer(dx, dy),
                device_id_type=MESH,
            )
            copy.start()
            sent.append(copy)
    for copy in sent:
        copy.wait_recv()

    before = [to_own[0], to_own[1], to_own[2]]
    for dy in range(ny):
        if dy:
            before = [before[i] + from_own[dy, i] for i in range(3)]
        before[0] = before[0] + from_low[dy, 1]
        before[1] = before[1] + from_low[dy, 0] + from_high[dy, 0]
        before[2] = before[2] + from_high[dy, 1]
    for xo in range(3):
        tile = before[xo] * COARSE_SCALE
        short = 128 - tile.shape[0]
        if short:
            tile = jnp.concatenate([tile, jnp.zeros((short, 128), jnp.float32)], axis=0)
        turned = tile.T
        for yo in range(3):
            for zo in range(3):
                coarse_ref[9 * xo + 3 * yo + zo, 0] = turned[
                    zo * count_z : (zo + 1) * count_z, yo * count_y : (yo + 1) * count_y
                ]

    for copy in copies.values():
        copy.wait_send()
    for copy in sent:
        copy.wait_send()
    stored.wait()


def shards(classes, support_mask):
    nx, ny = lax.axis_size("gx"), lax.axis_size("gy")
    width, rows, depth = classes.shape
    wide, deep = rows + EDGE, width + 2 * HALO
    count_y, count_z = rows * ny // 8, depth // 8
    lines = 3 * count_y
    partners = 3 * ny - 1
    halos = 5 if ny == 2 else 8
    plane = lambda *lead: pltpu.VMEM((*lead, wide, depth), jnp.float32)
    return pl.pallas_call(
        functools.partial(kernel, nx, ny),
        out_shape=(
            jax.ShapeDtypeStruct((8, width, rows, depth), jnp.float32),
            jax.ShapeDtypeStruct((27, 1, count_z, count_y), jnp.float32),
        ),
        in_specs=[pl.BlockSpec(memory_space=pl.ANY)] * 2,
        out_specs=(
            pl.BlockSpec(memory_space=pl.ANY),
            pl.BlockSpec(memory_space=pltpu.VMEM),
        ),
        scratch_shapes=[
            pltpu.VMEM((2, deep, wide, depth), jnp.int32),
            pltpu.VMEM((2, width, EDGE, depth), jnp.int32),
            pltpu.VMEM((2, 2, deep, EDGE, depth) if ny > 2 else (1, 1, 1, EDGE, depth), jnp.int32),
            plane(deep),
            plane(deep),
            plane(deep),
            plane(deep),
            plane(deep),
            plane(4),
            plane(8, deep),
            plane(8, deep),
            pltpu.VMEM((8, width, rows, depth), jnp.float32),
            pltpu.VMEM((8, 4 * rows, 4 * depth), jnp.float32),
            pltpu.VMEM((lines, 4 * rows), jnp.bfloat16),
            pltpu.VMEM((4 * depth, 128), jnp.bfloat16),
            pltpu.VMEM((8, lines, 128), jnp.float32),
            pltpu.VMEM((2, lines, 128), jnp.float32),
            pltpu.VMEM((2, lines, 128), jnp.float32),
            pltpu.VMEM((3, lines, 128), jnp.float32),
            pltpu.VMEM((ny, 2, lines, 128), jnp.float32),
            pltpu.VMEM((ny, 2, lines, 128), jnp.float32),
            pltpu.VMEM((ny, 3, lines, 128), jnp.float32),
            pltpu.SemaphoreType.DMA((2,)),
            pltpu.SemaphoreType.DMA((halos,)),
            pltpu.SemaphoreType.DMA((halos,)),
            pltpu.SemaphoreType.DMA((partners,)),
            pltpu.SemaphoreType.DMA((partners,)),
            pltpu.SemaphoreType.DMA,
        ],
        compiler_params=pltpu.CompilerParams(
            collective_id=0, has_side_effects=True, vmem_limit_bytes=32 * 1024 * 1024
        ),
    )(classes, support_mask)


def solution(mesh):
    in_specs = (P("gx", "gy", None), P("gx", "gy", None))
    out_specs = (P(None, "gx", "gy", None), P(None, "gx", None, None))
    return jax.shard_map(shards, mesh=mesh, in_specs=in_specs, out_specs=out_specs, check_vma=False)
```

time: 126 us -> 30.7 us (0.24); the launches traced: 125 us -> 30.5 us
  starting transfers between devices: 31.9 us -> 0 us
  other arithmetic: 28.6 us -> 0 us
  Pallas kernels: 0 us -> 26.3 us
  local copies, waits for them, and re-layouts: 29.1 us -> 3.57 us
  matrix products: 17.6 us -> 0 us
  waiting for transfers between devices: 12 us -> 0 us
  blocking collectives: 4.3 us -> 0 us
    ppermute x18 -> x0, starting transfers between devices: 31.9 us -> none  [the longest x9 28.1 us: extended(): after = lax.ppermute(first, axis, down)]
    pallas_call x0 -> x1, Pallas kernels: none -> 26.3 us  [shards(): pl.pallas_call(functools.partial(kernel, nx, ny), out_shape=(jax.ShapeDty...]
    mul x31 -> x0, local copies, waits for them, and re-layouts: 18.4 us -> none  [the longest x30 18.3 us: axis_table(): lines[:, :, None] * offset[:, None, :]]
    dot_general x24 -> x0, matrix products: 17.6 us -> none  [the longest x8 7.78 us: coarse_terms(): jnp.einsum('abexyz,ezk->abxyk', product, tables_third[c & 1], precision=H...]
    ppermute x18 -> x0, waiting for transfers between devices: 12 us -> none  [the longest x9 11.3 us: extended(): before = lax.ppermute(last, axis, up)]
    unnamed x11 -> x0, other arithmetic: 7.06 us -> none
    convert_element_type x13 -> x0, other arithmetic: 6.84 us -> none  [the longest x6 3.78 us: axis_table(): (row_index[:, None] == jnp.arange(rows, dtype=jnp.int32)[None, :]).astype...]
    slice x14 -> x0, local copies, waits for them, and re-layouts: 6.15 us -> none  [the longest x4 3.8 us: neighbours(): jnp.roll(centre, 1, 3)]
  transfers between devices with their start and end apart: 18 -> 0, of which waited for: 9 -> 0; matrix products, arithmetic and copies ran while one was open for 30% -> 0% of each run, Pallas kernels for 0% -> 0%
where the time goes in v1:
time: 30.7 us; the launch traced here: 30.5 us
  Pallas kernels  26.3 us (86%)
  local copies, waits for them, and re-layouts  3.57 us (12%)
  between operations  0.65 us (2%)
    pallas_call x1, Pallas kernels, shards(): pl.pallas_call(functools.partial(kernel, nx, ny), out_shape=(jax.ShapeDty...  26.3 us
    unnamed x5, local copies, waits for them, and re-layouts  2.77 us
    pallas_call x1, local copies, waits for them, and re-layouts, shards(): pl.pallas_call(functools.partial(kernel, nx, ny), out_shape=(jax.ShapeDty...  0.8 us

profile of v1, /device:TPU:0, one launch (start us, length us, event | category | flops | bytes accessed | tf_op | source)
XLA Modules:
  0.0 30.5 jit_solution(17223830252423574111)
XLA Ops:
  0.6 0.0 copy-start
  0.6 0.9 %copy-done = s32[8,32,128]{2,1,0:T(8,128)S(1)} copy-done((s32[8,32,128]{2,1,0:T(8,128)S(1)}, s32[8,32,128]{2,1,0:T(8,128)}, u32[]{:S(2)}) %copy-start) | copy-done | bytes 131096
  1.5 0.0 copy-start.1
  1.5 0.9 %copy-done.1 = s32[8,32,128]{2,1,0:T(8,128)S(1)} copy-done((s32[8,32,128]{2,1,0:T(8,128)S(1)}, s32[8,32,128]{2,1,0:T(8,128)}, u32[]{:S(2)}) %copy-start.1) | copy-done | bytes 131096
  2.4 26.3 %shard_map.41 = (f32[8,8,32,128]{3,2,1,0:T(8,128)S(1)}, f32[27,1,16,8]{3,2,1,0:T(8,128)S(1)}) custom-call(s32[8,32,128]{2,1,0:T(8,128)S(1)} %copy-done, s32[8,32,128]{2,1,0:T(8,128)S(1)} %copy-done.1), custom_call_target="tpu_custom_call" | custom-call | tf_op jit(solution)/shard_map/pallas_call | solution.py:415
  28.8 0.8 %copy.4 = f32[27,1,16,8]{0,3,2,1:T(8,128)} copy(f32[27,1,16,8]{3,2,1,0:T(8,128)S(1)} %get-tuple-element.3) | data formatting | bytes 27648 | tf_op jit(solution)/shard_map/pallas_call | solution.py:415
  29.6 1.0 %copy.6 = f32[8,8,32,128]{3,2,1,0:T(8,128)} copy(f32[8,8,32,128]{3,2,1,0:T(8,128)S(1)} %get-tuple-element.6) | data formatting | bytes 2097152
Async XLA Ops:
  0.6 0.9 %copy-start = (s32[8,32,128]{2,1,0:T(8,128)S(1)}, s32[8,32,128]{2,1,0:T(8,128)}, u32[]{:S(2)}) copy-start(s32[8,32,128]{2,1,0:T(8,128)} %cls_hbm.1) | copy-start | bytes 393220
  1.5 0.9 %copy-start.1 = (s32[8,32,128]{2,1,0:T(8,128)S(1)}, s32[8,32,128]{2,1,0:T(8,128)}, u32[]{:S(2)}) copy-start(s32[8,32,128]{2,1,0:T(8,128)} %msk_hbm.1) | copy-start | bytes 393220

commit v2 on v1

--- a/solution.py
+++ b/solution.py
@@ -17,6 +17,10 @@
     blocks = places >> 3
     same = (blocks & 1) == chosen
     return jnp.where(same, blocks, jnp.where((places & 7) < 4, blocks - 1, blocks + 1))
+
+
+def wrap(node, count):
+    return jnp.where(node < 0, node + count, jnp.where(node >= count, node - count, node))
 
 
 def weight_of(places, chosen):
@@ -44,8 +48,7 @@
 def kernel(
     nx,
     ny,
-    cls_hbm,
-    msk_hbm,
+    both_hbm,
     basis_hbm,
     coarse_ref,
     cells,
@@ -77,7 +80,7 @@
     term_recv,
     out_sem,
 ):
-    width, rows, depth = cls_hbm.shape
+    _, width, rows, depth = both_hbm.shape
     wide = rows + EDGE
     count_y = rows * ny // 8
     count_z = depth // 8
@@ -90,10 +93,7 @@
     def peer(dx, dy):
         return (lax.rem(gx + dx + nx, nx), lax.rem(gy + dy + ny, ny))
 
-    loads = [
-        pltpu.make_async_copy(ref, cells.at[i, own, main, :], load_sem.at[i])
-        for i, ref in enumerate((cls_hbm, msk_hbm))
-    ]
+    loads = [pltpu.make_async_copy(both_hbm, cells.at[:, own, main, :], load_sem.at[0])]
     for copy in loads:
         copy.start()
 
@@ -101,31 +101,6 @@
     barrier = pltpu.get_barrier_semaphore()
     for dx, dy in partners:
         pl.semaphore_signal(barrier, inc=1, device_id=peer(dx, dy), device_id_type=MESH)
-
-    row_pos = lax.broadcasted_iota(jnp.int32, (wide, depth), 0)
-    second = gy * rows + jnp.where(row_pos < rows + EDGE // 2, row_pos, row_pos - wide)
-    third = lax.broadcasted_iota(jnp.int32, (wide, depth), 1)
-    for b in (0, 1):
-        for e in (0, 1):
-            plane_w[2 * b + e] = weight_of(second, b) * weight_of(third, e)
-    place = lax.broadcasted_iota(jnp.int32, (depth, 128), 0)
-    lane = lax.broadcasted_iota(jnp.int32, (depth, 128), 1)
-    for e in (0, 1):
-        for other in (0, 1):
-            mine = node_of(place, e)
-            shift = node_of(place, other) - mine + 1
-            column = lax.rem(mine + count_z, count_z) + count_z * shift
-            table_z[pl.ds((2 * e + other) * depth, depth), :] = jnp.where(
-                column == lane, 1.0, 0.0
-            ).astype(jnp.bfloat16)
-    line = lax.broadcasted_iota(jnp.int32, table_y.shape, 0)
-    column = lax.broadcasted_iota(jnp.int32, table_y.shape, 1)
-    bits = column // rows
-    spot = gy * rows + column - rows * bits
-    mine = jnp.where(bits >= 2, node_of(spot, 1), node_of(spot, 0))
-    theirs = jnp.where((bits & 1) == 1, node_of(spot, 1), node_of(spot, 0))
-    target = lax.rem(mine + count_y, count_y) + count_y * (theirs - mine + 1)
-    table_y[...] = jnp.where(target == line, 1.0, 0.0).astype(jnp.bfloat16)
 
     for copy in loads:
         copy.wait()
@@ -158,15 +133,17 @@
         -1: (0, HALO + width, HALO),
         1: (width - HALO, 0, HALO),
     }
-    for dx in (1, -1):
-        start, land, size = spans[dx]
-        send(
-            ("x", dx),
-            cells.at[:, pl.ds(HALO + start, size), main, :],
-            cells.at[:, pl.ds(land, size), main, :],
-            dx,
-            0,
-        )
+    for i in (0, 1):
+        for p in range(HALO):
+            for dx in (1, -1):
+                start, land, size = spans[dx]
+                send(
+                    ("x", dx, i, p),
+                    cells.at[i, HALO + start + p, main, :],
+                    cells.at[i, land + p, main, :],
+                    dx,
+                    0,
+                )
     for dx in (1, -1, 0):
         start, land, size = spans[dx]
         if dx == 0:
@@ -189,12 +166,39 @@
                     dy,
                 )
 
+    row_pos = lax.broadcasted_iota(jnp.int32, (wide, depth), 0)
+    second = gy * rows + jnp.where(row_pos < rows + EDGE // 2, row_pos, row_pos - wide)
+    third = lax.broadcasted_iota(jnp.int32, (wide, depth), 1)
+    for b in (0, 1):
+        for e in (0, 1):
+            plane_w[2 * b + e] = weight_of(second, b) * weight_of(third, e)
+    place = lax.broadcasted_iota(jnp.int32, (depth, 128), 0)
+    lane = lax.broadcasted_iota(jnp.int32, (depth, 128), 1)
+    for e in (0, 1):
+        for other in (0, 1):
+            mine = node_of(place, e)
+            shift = node_of(place, other) - mine + 1
+            column = wrap(mine, count_z) + count_z * shift
+            table_z[pl.ds((2 * e + other) * depth, depth), :] = jnp.where(
+                column == lane, 1.0, 0.0
+            ).astype(jnp.bfloat16)
+    line = lax.broadcasted_iota(jnp.int32, table_y.shape, 0)
+    column = lax.broadcasted_iota(jnp.int32, table_y.shape, 1)
+    bits = column // rows
+    spot = gy * rows + column - rows * bits
+    mine = jnp.where(bits >= 2, node_of(spot, 1), node_of(spot, 0))
+    theirs = jnp.where((bits & 1) == 1, node_of(spot, 1), node_of(spot, 0))
+    target = wrap(mine, count_y) + count_y * (theirs - mine + 1)
+    table_y[...] = jnp.where(target == line, 1.0, 0.0).astype(jnp.bfloat16)
+
     def receive(dx):
         _, land, size = spans[dx]
         if dx == 0:
             land = HALO
         else:
-            copies[("x", dx)].wait_recv()
+            for i in (0, 1):
+                for p in range(HALO):
+                    copies[("x", dx, i, p)].wait_recv()
         if ny == 2:
             copies[("y", dx, 0)].wait_recv()
         else:
@@ -290,70 +294,82 @@
             work(x)
             return carry
 
-        lax.fori_loop(first, last, body, 0)
-
-    def outer(work, low, high, size=HALO):
+        lax.fori_loop(first, last, body, 0, unroll=2)
+
+    def beside(work, low, high, upper):
         def body(i, carry):
-            work(i + low + (i // size) * (high - low - size))
+            work(i + low + upper * (high - low))
             return carry
 
-        lax.fori_loop(0, 2 * size, body, 0)
+        lax.fori_loop(0, HALO, body, 0, unroll=True)
 
     top = HALO + width
+    first_step = functools.partial(smooth, phi_a, phi_b)
+    second_step = functools.partial(smooth, phi_b, phi_a)
+    operator = functools.partial(apply, phi_a)
     receive(0)
     inner(prepare, HALO, top)
     inner(join, HALO, top - 1)
     inner(gather, HALO + 1, top - 1)
-    inner(functools.partial(smooth, phi_a, phi_b), HALO + 1, top - 1)
-
-    receive(1)
-    receive(-1)
-    outer(prepare, 0, top)
-    outer(join, 0, top - 1)
-    outer(gather, 1, top - 1)
-    outer(functools.partial(smooth, phi_a, phi_b), 1, top - 1)
-    inner(functools.partial(smooth, phi_b, phi_a), HALO - 1, top + 1)
+    inner(first_step, HALO + 1, top - 1)
+    inner(second_step, HALO + 2, top - 2)
+    inner(operator, HALO + 3, top - 3)
+
+    tiles = rows // 8
+
+    def products(half):
+        def body(step, carry):
+            tile = pl.multiple_of(step * 8, 8)
+            at = pl.ds(tile, 8)
+            for c_half in range(2):
+                total = {}
+                for i in range(width // 2):
+                    x = half * (width // 2) + i
+                    images = [image[d, x, at, :] for d in range(8)]
+                    for c in range(4 * c_half, 4 * c_half + 4):
+                        field = phi_a[c, x + HALO, at, :]
+                        for d in range(8):
+                            value = field * images[d]
+                            total[c, d] = value if i == 0 else total[c, d] + value
+                for (c, d), value in total.items():
+                    group = (c >> 2) * 2 + (d >> 2)
+                    block = group * 4 + (c >> 1 & 1) * 2 + (d >> 1 & 1)
+                    column = (c & 1) * 2 + (d & 1)
+                    pairs[pl.ds(block * rows + tile, 8), pl.ds(column * depth, depth)] = value
+            return carry
+
+        lax.fori_loop(0, tiles, body, 0)
+        section = split_dot(pairs[...], table_z[...], False)
+        for group in range(4):
+            part = section[group * 4 * rows : (group + 1) * 4 * rows]
+            terms[half, group] = split_dot(table_y[...], part, True)
+
+    for upper in (1 - parity, parity):
+        @pl.when(upper == 1)
+        def _():
+            receive(-1)
+
+        @pl.when(upper == 0)
+        def _():
+            receive(1)
+
+        beside(prepare, 0, top, upper)
+        beside(join, 0, top - 1, upper)
+        beside(gather, 1, top - 1, upper)
+        beside(first_step, 1, top - 1, upper)
+        beside(second_step, 2, top - 2, upper)
+        beside(operator, 3, top - 3, upper)
+        products(upper)
+
     stored = pltpu.make_async_copy(phi_a.at[:, own, main, :], basis_hbm, out_sem)
     stored.start()
-    inner(functools.partial(apply, phi_a), HALO, top)
-
-    tiles = rows // 8
-
-    def products(step, carry):
-        half = step // tiles
-        tile = pl.multiple_of(lax.rem(step, tiles) * 8, 8)
-        at = pl.ds(tile, 8)
-        for c_half in range(2):
-            total = {}
-            for i in range(width // 2):
-                x = half * (width // 2) + i
-                images = [image[d, x, at, :] for d in range(8)]
-                for c in range(4 * c_half, 4 * c_half + 4):
-                    field = phi_a[c, x + HALO, at, :]
-                    for d in range(8):
-                        value = field * images[d]
-                        total[c, d] = value if i == 0 else total[c, d] + value
-            for (c, d), value in total.items():
-                group = ((c >> 2) * 2 + (d >> 2)) * 2 + half
-                block = (c >> 1 & 1) * 2 + (d >> 1 & 1)
-                column = (c & 1) * 2 + (d & 1)
-                pairs[group, pl.ds(block * rows + tile, 8), pl.ds(column * depth, depth)] = value
-        return carry
-
-    lax.fori_loop(0, 2 * tiles, products, 0)
-
-    for group in range(8):
-        section = split_dot(pairs[group], table_z[...], False)
-        terms[group] = split_dot(table_y[...], section, True)
 
     def term(a, other, half):
-        return terms[(a * 2 + other) * 2 + half]
+        return terms[half, a * 2 + other]
 
     mine, off = parity, 1 - parity
-    to_low[0] = term(off, off, 0)
-    to_low[1] = term(off, mine, 0)
-    to_high[0] = term(off, off, 1)
-    to_high[1] = term(off, mine, 1)
+    to_low[...] = term(off, off, 0) + pltpu.roll(term(off, mine, 0), 64, 1)
+    to_high[...] = term(off, off, 1) + pltpu.roll(term(off, mine, 1), 64, 1)
     to_own[0] = term(mine, off, 0)
     to_own[1] = term(mine, mine, 0) + term(mine, mine, 1)
     to_own[2] = term(mine, off, 1)
@@ -381,9 +397,9 @@
     for dy in range(ny):
         if dy:
             before = [before[i] + from_own[dy, i] for i in range(3)]
-        before[0] = before[0] + from_low[dy, 1]
-        before[1] = before[1] + from_low[dy, 0] + from_high[dy, 0]
-        before[2] = before[2] + from_high[dy, 1]
+        before[0] = before[0] + pltpu.roll(from_low[dy], 64, 1)
+        before[1] = before[1] + from_low[dy] + from_high[dy]
+        before[2] = before[2] + pltpu.roll(from_high[dy], 64, 1)
     for xo in range(3):
         tile = before[xo] * COARSE_SCALE
         short = 128 - tile.shape[0]
@@ -410,7 +426,7 @@
     count_y, count_z = rows * ny // 8, depth // 8
     lines = 3 * count_y
     partners = 3 * ny - 1
-    halos = 5 if ny == 2 else 8
+    halos = 4 * HALO + (3 if ny == 2 else 6)
     plane = lambda *lead: pltpu.VMEM((*lead, wide, depth), jnp.float32)
     return pl.pallas_call(
         functools.partial(kernel, nx, ny),
@@ -418,7 +434,7 @@
             jax.ShapeDtypeStruct((8, width, rows, depth), jnp.float32),
             jax.ShapeDtypeStruct((27, 1, count_z, count_y), jnp.float32),
         ),
-        in_specs=[pl.BlockSpec(memory_space=pl.ANY)] * 2,
+        in_specs=[pl.BlockSpec(memory_space=pl.ANY)],
         out_specs=(
             pl.BlockSpec(memory_space=pl.ANY),
             pl.BlockSpec(memory_space=pltpu.VMEM),
@@ -436,15 +452,15 @@
             plane(8, deep),
             plane(8, deep),
             pltpu.VMEM((8, width, rows, depth), jnp.float32),
-            pltpu.VMEM((8, 4 * rows, 4 * depth), jnp.float32),
+            pltpu.VMEM((16 * rows, 4 * depth), jnp.float32),
             pltpu.VMEM((lines, 4 * rows), jnp.bfloat16),
             pltpu.VMEM((4 * depth, 128), jnp.bfloat16),
-            pltpu.VMEM((8, lines, 128), jnp.float32),
-            pltpu.VMEM((2, lines, 128), jnp.float32),
-            pltpu.VMEM((2, lines, 128), jnp.float32),
+            pltpu.VMEM((2, 4, lines, 128), jnp.float32),
+            pltpu.VMEM((lines, 128), jnp.float32),
+            pltpu.VMEM((lines, 128), jnp.float32),
             pltpu.VMEM((3, lines, 128), jnp.float32),
-            pltpu.VMEM((ny, 2, lines, 128), jnp.float32),
-            pltpu.VMEM((ny, 2, lines, 128), jnp.float32),
+            pltpu.VMEM((ny, lines, 128), jnp.float32),
+            pltpu.VMEM((ny, lines, 128), jnp.float32),
             pltpu.VMEM((ny, 3, lines, 128), jnp.float32),
             pltpu.SemaphoreType.DMA((2,)),
             pltpu.SemaphoreType.DMA((halos,)),
@@ -456,7 +472,7 @@
         compiler_params=pltpu.CompilerParams(
             collective_id=0, has_side_effects=True, vmem_limit_bytes=32 * 1024 * 1024
         ),
-    )(classes, support_mask)
+    )(jnp.stack([classes, support_mask]))
 
 
 def solution(mesh):

time: 30.7 us -> 26.2 us (0.85)
  Pallas kernels: 26.3 us -> 22.7 us
  local copies, waits for them, and re-layouts: 3.57 us -> 1.77 us
  other arithmetic: 0 us -> 0.99 us
    pallas_call x1, Pallas kernels: 26.3 us -> 22.7 us  [shards(): pl.pallas_call(functools.partial(kernel, nx, ny), out_shape=(jax.ShapeDty...]
    unnamed x5 -> x1, local copies, waits for them, and re-layouts: 2.77 us -> 0.97 us
    another operation x0 -> x1, other arithmetic: none -> 0.99 us  [shards(): jnp.stack([classes, support_mask])]
where the time goes in v2:
time: 26.2 us; the launch traced here: 26.1 us
  Pallas kernels  22.7 us (87%)
  local copies, waits for them, and re-layouts  1.77 us (7%)
  other arithmetic  0.99 us (4%)
  between operations  0.64 us (2%)
    pallas_call x1, Pallas kernels, shards(): pl.pallas_call(functools.partial(kernel, nx, ny), out_shape=(jax.ShapeDty...  22.7 us
    another operation x1, other arithmetic, shards(): jnp.stack([classes, support_mask])  0.99 us
    unnamed x1, local copies, waits for them, and re-layouts  0.97 us
    pallas_call x1, local copies, waits for them, and re-layouts, shards(): pl.pallas_call(functools.partial(kernel, nx, ny), out_shape=(jax.ShapeDty...  0.8 us

profile of v2, /device:TPU:0, one launch (start us, length us, event | category | flops | bytes accessed | tf_op | source)
XLA Modules:
  0.0 26.1 jit_solution(5157447897191874017)
XLA Ops:
  0.6 1.0 %pad_add_fusion.both_hbm = s32[2,8,32,128]{3,2,1,0:T(8,128)S(1)} fusion(s32[1,8,32,128]{3,2,1,0:T(8,128)} %bitcast.2, s32[1,8,32,128]{3,2,1,0:T(8,128)} %bitcast.3), kind=kLoop, calls=%fused_computation | loop fusion | flops 65536 | bytes 524288 | tf_op jit(solution)/shard_map/stack | solution.py:475
  1.6 22.7 %shard_map.41 = (f32[8,8,32,128]{3,2,1,0:T(8,128)S(1)}, f32[27,1,16,8]{3,2,1,0:T(8,128)S(1)}) custom-call(s32[2,8,32,128]{3,2,1,0:T(8,128)S(1)} %pad_add_fusion.both_hbm), custom_call_target="tpu_custom_call" | custom-call | tf_op jit(solution)/shard_map/pallas_call | solution.py:431
  24.3 0.8 %copy.4 = f32[27,1,16,8]{0,3,2,1:T(8,128)} copy(f32[27,1,16,8]{3,2,1,0:T(8,128)S(1)} %get-tuple-element.3) | data formatting | bytes 27648 | tf_op jit(solution)/shard_map/pallas_call | solution.py:431
  25.1 1.0 %copy.6 = f32[8,8,32,128]{3,2,1,0:T(8,128)} copy(f32[8,8,32,128]{3,2,1,0:T(8,128)S(1)} %get-tuple-element.6) | data formatting | bytes 2097152

commit v3 on v2

--- a/solution.py
+++ b/solution.py
@@ -344,38 +344,14 @@
             part = section[group * 4 * rows : (group + 1) * 4 * rows]
             terms[half, group] = split_dot(table_y[...], part, True)
 
-    for upper in (1 - parity, parity):
-        @pl.when(upper == 1)
-        def _():
-            receive(-1)
-
-        @pl.when(upper == 0)
-        def _():
-            receive(1)
-
-        beside(prepare, 0, top, upper)
-        beside(join, 0, top - 1, upper)
-        beside(gather, 1, top - 1, upper)
-        beside(first_step, 1, top - 1, upper)
-        beside(second_step, 2, top - 2, upper)
-        beside(operator, 3, top - 3, upper)
-        products(upper)
-
-    stored = pltpu.make_async_copy(phi_a.at[:, own, main, :], basis_hbm, out_sem)
-    stored.start()
-
     def term(a, other, half):
         return terms[half, a * 2 + other]
 
     mine, off = parity, 1 - parity
-    to_low[...] = term(off, off, 0) + pltpu.roll(term(off, mine, 0), 64, 1)
-    to_high[...] = term(off, off, 1) + pltpu.roll(term(off, mine, 1), 64, 1)
-    to_own[0] = term(mine, off, 0)
-    to_own[1] = term(mine, mine, 0) + term(mine, mine, 1)
-    to_own[2] = term(mine, off, 1)
-
     sent = []
-    for source, landing, dx in ((to_low, from_high, -1), (to_high, from_low, 1), (to_own, from_own, 0)):
+
+    def outgoing(source, landing, dx):
+        group = []
         for dy in range(ny):
             if (dx, dy) == (0, 0):
                 continue
@@ -388,8 +364,51 @@
                 device_id=peer(dx, dy),
                 device_id_type=MESH,
             )
-            copy.start()
+            group.append(copy)
             sent.append(copy)
+        return group
+
+    low_copies = outgoing(to_low, from_high, -1)
+    high_copies = outgoing(to_high, from_low, 1)
+    own_copies = outgoing(to_own, from_own, 0)
+
+    for upper in (1 - parity, parity):
+        @pl.when(upper == 1)
+        def _():
+            receive(-1)
+
+        @pl.when(upper == 0)
+        def _():
+            receive(1)
+
+        beside(prepare, 0, top, upper)
+        beside(join, 0, top - 1, upper)
+        beside(gather, 1, top - 1, upper)
+        beside(first_step, 1, top - 1, upper)
+        beside(second_step, 2, top - 2, upper)
+        beside(operator, 3, top - 3, upper)
+        products(upper)
+
+        @pl.when(upper == 1)
+        def _():
+            to_high[...] = term(off, off, 1) + pltpu.roll(term(off, mine, 1), 64, 1)
+            for copy in high_copies:
+                copy.start()
+
+        @pl.when(upper == 0)
+        def _():
+            to_low[...] = term(off, off, 0) + pltpu.roll(term(off, mine, 0), 64, 1)
+            for copy in low_copies:
+                copy.start()
+
+    to_own[0] = term(mine, off, 0)
+    to_own[1] = term(mine, mine, 0) + term(mine, mine, 1)
+    to_own[2] = term(mine, off, 1)
+    for copy in own_copies:
+        copy.start()
+    stored = pltpu.make_async_copy(phi_a.at[:, own, main, :], basis_hbm, out_sem)
+    stored.start()
+
     for copy in sent:
         copy.wait_recv()
 

time: 26.2 us -> 26.1 us (level)
  no operation moved by 1% of the time
where the time goes in v3:
time: 26.1 us; the launch traced here: 26 us
  Pallas kernels  22.6 us (87%)
  local copies, waits for them, and re-layouts  1.77 us (7%)
  other arithmetic  0.99 us (4%)
  between operations  0.64 us (2%)
    pallas_call x1, Pallas kernels, shards(): pl.pallas_call(functools.partial(kernel, nx, ny), out_shape=(jax.ShapeDty...  22.6 us
    another operation x1, other arithmetic, shards(): jnp.stack([classes, support_mask])  0.99 us
    unnamed x1, local copies, waits for them, and re-layouts  0.97 us
    pallas_call x1, local copies, waits for them, and re-layouts, shards(): pl.pallas_call(functools.partial(kernel, nx, ny), out_shape=(jax.ShapeDty...  0.8 us

profile of v3, /device:TPU:0, one launch (start us, length us, event | category | flops | bytes accessed | tf_op | source)
XLA Modules:
  0.0 26.0 jit_solution(14204843526322093875)
XLA Ops:
  0.6 1.0 %pad_add_fusion.both_hbm = s32[2,8,32,128]{3,2,1,0:T(8,128)S(1)} fusion(s32[1,8,32,128]{3,2,1,0:T(8,128)} %bitcast.2, s32[1,8,32,128]{3,2,1,0:T(8,128)} %bitcast.3), kind=kLoop, calls=%fused_computation | loop fusion | flops 65536 | bytes 524288 | tf_op jit(solution)/shard_map/stack | solution.py:494
  1.6 22.6 %shard_map.41 = (f32[8,8,32,128]{3,2,1,0:T(8,128)S(1)}, f32[27,1,16,8]{3,2,1,0:T(8,128)S(1)}) custom-call(s32[2,8,32,128]{3,2,1,0:T(8,128)S(1)} %pad_add_fusion.both_hbm), custom_call_target="tpu_custom_call" | custom-call | tf_op jit(solution)/shard_map/pallas_call | solution.py:450
  24.2 0.8 %copy.4 = f32[27,1,16,8]{0,3,2,1:T(8,128)} copy(f32[27,1,16,8]{3,2,1,0:T(8,128)S(1)} %get-tuple-element.3) | data formatting | bytes 27648 | tf_op jit(solution)/shard_map/pallas_call | solution.py:450
  25.0 1.0 %copy.6 = f32[8,8,32,128]{3,2,1,0:T(8,128)} copy(f32[8,8,32,128]{3,2,1,0:T(8,128)S(1)} %get-tuple-element.6) | data formatting | bytes 2097152
